TPU v7x, 32 devices: a whole 2x2x4 slice. The times are simulated.
32 devices in a mesh: ctx: 8 (over z, x), ch: 4 (over y, core).
Axes of the slice: x: 2, y: 2, z: 4, core: 2. Of those that a mesh axis runs over, the one named last changes fastest.
Arguments:
- streams: bfloat16 [2048, 3, 4096], P('ctx', None, 'ch'), may hold values from -6 to 6
- feat_weight: float32 [3, 7, 4096], P(None, None, 'ch'), may hold values from -2 to 2
- skip_gain: float32 [4096], P('ch'), may hold values from -4 to 4
- spectrum_values: bfloat16 [2, 16, 256, 512], P(None, 'ctx', None, 'ch'), as said below
- spectrum_scales: float32 [16, 2, 512], P('ctx', None, 'ch'), may hold values from 0.25 to 4, as said below
- group_filter: int32 [256], replicated, may hold values from 0 to 511
- doc_lengths: int32 [32], replicated, may hold values from 1 to 512, 2048 in all
Outputs:
- mixed: bfloat16 [2048, 4096], P('ctx', 'ch')
Inputs may be any that keep to these rules, and one draw needn't show every extreme that they name: `group_filter`: the filter index of each group of 16 neighbouring channels. `doc_lengths`: document lengths in sequence order, summing to 2048. `spectrum_values`: the spectra are those of real filters: the stored value at frequency 2 * 2048 - k is the complex conjugate of the value at k. `spectrum_scales`: frequencies k and 4096 - k have the same scale.
All inputs are finite; a program needn't handle non-finite values.
Results may differ from a plain program's by a relative error of at most 0.0085.
Values may be sent and summed in bfloat16 or wider, within the bound.
A program may use at most 64 MiB of HBM per device.

v0:
```python
import math

import jax
import jax.numpy as jnp
import numpy as np
from jax import lax
from jax.sharding import PartitionSpec as P

GROUP_CH = 16
FEAT_TAPS = 7
SCALE_BLOCK = 128


def from_behind(shard, axis, by):
    size = lax.axis_size(axis)
    pairs = [(i, i + by) for i in range(size) if 0 <= i + by < size]
    return lax.ppermute(shard, axis, pairs)


def wave(rows, cols, period):
    angle = np.outer(rows, cols) % period * (2.0 * math.pi / period)
    return np.cos(angle), np.sin(angle)


def featurize(streams, rim, feat_weight, doc_lengths, ctx_index):
    tokens = streams.shape[0]
    reach = FEAT_TAPS - 1
    extended = jnp.concatenate([rim, streams], axis=0).astype(jnp.float32)
    positions = ctx_index * tokens + jnp.arange(tokens, dtype=jnp.int32)
    ends = jnp.cumsum(doc_lengths)
    begins = jnp.max(jnp.where(positions[:, None] >= ends[None, :], ends[None, :], 0), axis=1)
    inside = positions - begins
    featured = jnp.zeros((tokens,) + streams.shape[1:], jnp.float32)
    for tap_index in range(FEAT_TAPS):
        start = reach - tap_index
        source = extended[start : start + tokens]
        same = inside >= tap_index
        featured = featured + jnp.where(
            same[:, None, None], feat_weight[:, tap_index, :][None] * source, 0.0
        )
    return featured[:, 0], featured[:, 1] * featured[:, 2]


def long_conv(columns, spec_real, spec_imag, ctx_count):
    tokens = columns.shape[1]
    total_len = 2 * tokens * ctx_count
    outer = np.arange(ctx_count + 1)
    cos_o, sin_o = wave(outer, np.arange(ctx_count), 2 * ctx_count)
    cos_t, sin_t = wave(outer, np.arange(tokens), total_len)
    cos_i, sin_i = wave(np.arange(tokens), np.arange(tokens), tokens)
    f32 = jnp.float32
    high = lax.Precision.HIGHEST
    xs = columns.astype(f32)
    u_real = jnp.einsum("ka,abc->kbc", jnp.asarray(cos_o, f32), xs, precision=high)
    u_imag = jnp.einsum("ka,abc->kbc", jnp.asarray(-sin_o, f32), xs, precision=high)
    ct, st = jnp.asarray(cos_t, f32)[:, :, None], jnp.asarray(sin_t, f32)[:, :, None]
    b_real = (u_real * ct + u_imag * st).astype(jnp.bfloat16)
    b_imag = (u_imag * ct - u_real * st).astype(jnp.bfloat16)
    table = jnp.asarray(np.concatenate([cos_i, sin_i], axis=0), jnp.bfloat16)

    def inner(real, imag):
        both = jnp.concatenate([real, imag], axis=2)
        out = jnp.einsum("qt,ktc->kqc", table, both, preferred_element_type=f32)
        width = real.shape[2]
        return (
            out[:, :tokens, :width],
            out[:, :tokens, width:],
            out[:, tokens:, :width],
            out[:, tokens:, width:],
        )

    cr, ci, sr, si = inner(b_real, b_imag)
    z_real, z_imag = cr + si, ci - sr
    p_real = (z_real * spec_real - z_imag * spec_imag).astype(jnp.bfloat16)
    p_imag = (z_real * spec_imag + z_imag * spec_real).astype(jnp.bfloat16)
    cr, ci, sr, si = inner(p_real, p_imag)
    v_real, v_imag = cr - si, ci + sr
    t_real = v_real * ct - v_imag * st
    t_imag = v_imag * ct + v_real * st
    weight = np.where((outer == 0) | (outer == ctx_count), 1.0, 2.0)[:, None] / total_len
    back_r = jnp.asarray(cos_o * weight, f32)
    back_i = jnp.asarray(-sin_o * weight, f32)
    return jnp.einsum("ka,kbc->abc", back_r, t_real, precision=high) + jnp.einsum(
        "ka,kbc->abc", back_i, t_imag, precision=high
    )


def per_device(
    streams, feat_weight, skip_gain, spectrum_values, spectrum_scales, group_filter, doc_lengths
):
    tokens = streams.shape[0]
    local_ch = streams.shape[2]
    ctx_count = lax.axis_size("ctx")
    reach = FEAT_TAPS - 1
    ctx_index = lax.axis_index("ctx")
    ch_index = lax.axis_index("ch")
    groups_local = local_ch // GROUP_CH
    scaled = spectrum_values.astype(jnp.float32) * jnp.repeat(spectrum_scales, SCALE_BLOCK, axis=1)
    bank = lax.all_gather(scaled.astype(jnp.bfloat16), "ch", axis=3, tiled=True)
    mine = lax.dynamic_slice_in_dim(group_filter, ch_index * groups_local, groups_local)
    onehot = jnp.arange(bank.shape[3], dtype=jnp.int32)[:, None] == mine[None, :]
    chosen = jnp.einsum(
        "rkqf,fg->kgrq", bank, onehot.astype(jnp.bfloat16), preferred_element_type=jnp.float32
    ).astype(jnp.bfloat16)
    rim = from_behind(streams[tokens - reach :], "ctx", 1)
    query, mixed_in = featurize(streams, rim, feat_weight, doc_lengths, ctx_index)
    columns = lax.all_to_all(
        mixed_in.astype(jnp.bfloat16), "ctx", split_axis=1, concat_axis=0, tiled=True
    ).reshape(ctx_count, tokens, -1)
    spec = lax.all_to_all(chosen, "ctx", split_axis=1, concat_axis=0, tiled=True)
    spec = jnp.concatenate([spec[0::2], spec[1:2]], axis=0)
    spec = jnp.repeat(jnp.transpose(spec, (2, 0, 3, 1)), GROUP_CH, axis=3).astype(jnp.float32)
    signal = long_conv(columns, spec[0], spec[1], ctx_count)
    conv = lax.all_to_all(
        signal.astype(jnp.bfloat16), "ctx", split_axis=0, concat_axis=2, tiled=True
    ).reshape(tokens, local_ch)
    conv = conv.astype(jnp.float32)
    return (query * (conv + skip_gain[None] * mixed_in)).astype(jnp.bfloat16)


def solution(mesh):
    placed = (
        P("ctx", None, "ch"),
        P(None, None, "ch"),
        P("ch"),
        P(None, "ctx", None, "ch"),
        P("ctx", None, "ch"),
        P(),
        P(),
    )
    return jax.shard_map(
        per_device, mesh=mesh, in_specs=placed, out_specs=P("ctx", "ch"), check_vma=False
    )
```

profile of v0, /device:TPU:0, one launch (start us, length us, event | category | flops | bytes accessed | tf_op | source)
XLA Modules:
  0.0 127.6 jit_solution(17090756698763221797)
XLA Ops:
  6.5 0.8 slice.99
  7.3 4.8 %collective-permute-start = (bf16[6,3,1024]{2,0,1:T(8,128)(2,1)S(1)}, bf16[6,3,1024]{2,0,1:T(8,128)(2,1)S(1)}, u32[]{:S(2)}, u32[]{:S(2)}) collective-permute-start(bf16[6,3,1024]{2,0,1:T(8,128)(2,1)S(1)} %slice.99), channel_id=1, source_target_pairs={{0,4},{4,8},{8,12},{12,16},{16,20},{20,24},{24,28},{1,5},{5,9},{9,... | collective-permute-start | bytes 110600 | tf_op jit(solution)/shard_map/ppermute | solution.py:17
  12.2 0.7 copy.54
  13.0 0.1 reduce-window.8
  13.0 0.1 reduce
  13.1 0.1 select_reduce_fusion
  13.2 1.5 %fusion.55 = (f32[3,1,1024]{2,1,0:T(1,128)S(1)}, f32[3,1,1024]{2,1,0:T(1,128)S(1)}, f32[3,1,1024]{2,1,0:T(1,128)S(1)}, f32[3,1,1024]{2,1,0:T(1,128)S(1)}, f32[3,...) fusion(f32[3,7,1024]{2,1,0:T(8,128)} %param.15), kind=kLoop, calls=%fused_computation.93 | loop fusion | bytes 172032 | tf_op jit(solution)/shard_map/slice | solution.py:39
  14.8 1.7 %copy.56 = bf16[256,3,1024]{0,2,1:T(8,128)(2,1)S(1)} copy(bf16[256,3,1024]{2,0,1:T(8,128)(2,1)} %param.14) | data formatting | bytes 3145728 | tf_op args[0]
  16.5 0.0 collective-permute-done
  16.5 0.4 copy.55
  17.0 1.0 maximum_convert_fusion
  18.0 8.4 %fusion.1 = f32[256,3,1024]{0,2,1:T(8,128)S(1)} fusion(f32[262,3,1024]{0,2,1:T(8,128)S(1)} %maximum_convert_fusion, f32[3,1024]{1,0:T(4,128)S(1)} %get-tuple-element.26, f32[3,1024]{1,0:T(4,128)S(1)} %get-tuple-element.27, f32[3,1024]{1,0:T(4,128)S(1)} %get-tuple-element.28, f32[3,1024]{1,0:T(4,128)S(1)} %get-tuple-element.29, ...), kind=kLoop, calls=%fused_computation.2 | loop fusion | flops 15728640 | bytes 25253632 | tf_op jit(solution)/shard_map/add | solution.py:38
  26.4 0.0 copy-start.9
  26.4 0.0 copy-start.1
  26.4 0.9 fusion.48
  27.3 2.1 %copy.57 = bf16[256,8,128]{2,0,1:T(8,128)(2,1)} copy(bf16[256,8,128]{0,2,1:T(8,128)(2,1)} %bitcast.86) | data formatting | bytes 1048576 | tf_op jit(solution)/shard_map/convert_element_type | solution.py:108
  29.4 4.9 %all-to-all-start = ((bf16[256,8,128]{2,0,1:T(8,128)(2,1)}), bf16[256,8,128]{2,0,1:T(8,128)(2,1)}, u32[]{:S(2)}, u32[]{:S(2)}) async-start(bf16[256,8,128]{2,0,1:T(8,128)(2,1)} %copy.57), calls=%async_computation | async-start | bytes 1048576 | tf_op jit(solution)/shard_map/all_to_all | solution.py:107
  34.3 0.0 copy-start.8
  34.3 0.0 all-gather.2.cloned.1.call-start
  34.3 0.0 copy-done.9
  34.4 0.8 multiply_convert_fusion
  35.2 0.0 all-gather.2.cloned.1.call-update
  35.2 0.1 dynamic_slice.3
  35.3 13.4 %all-to-all-done = bf16[256,8,128]{2,0,1:T(8,128)(2,1)} async-done(((bf16[256,8,128]{2,0,1:T(8,128)(2,1)}), bf16[256,8,128]{2,0,1:T(8,128)(2,1)}, u32[]{:S(2)}, u32[]{:S(2)}) %all-to-all-start) | async-done | bytes 524320 | tf_op jit(solution)/shard_map/all_to_all | solution.py:107
  48.6 2.1 %fusion.44 = f32[9,256,128]{2,0,1:T(8,128)S(1)} fusion(f32[9,8,1]{0,1,2:T(8,128)S(1)} %copy-done.6, bf16[256,8,128]{2,0,1:T(8,128)(2,1)} %all-to-all-done), kind=kOutput, calls=%fused_computation.62 | convolution fusion | flops 28311552 | bytes 1704224 | tf_op jit(solution)/shard_map/ka,abc->kbc/dot_general | solution.py:54
  50.8 3.1 %add_convert_fusion = (bf16[9,256,128]{2,0,1:T(8,128)(2,1)S(1)}, bf16[9,256,128]{2,0,1:T(8,128)(2,1)S(1)}) fusion(f32[9,256,128]{2,0,1:T(8,128)S(1)} %fusion.44, f32[9,256]{0,1:T(8,128)S(1)} %copy-done.2, f32[9,256]{0,1:T(8,128)S(1)} %copy-done.4, f32[9,8,1]{0,1,2:T(8,128)S(1)} %copy-done.8, bf16[256,8,128]{2,0,1:T(8,128)(2,1)} %all-to-all-done), kind=kOutput, calls=%fused_computation.34 | convolution fusion | flops 30670848 | bytes 2902304 | tf_op jit(solution)/shard_map/ka,abc->kbc/dot_general | solution.py:55
  53.9 0.0 copy-start
  53.9 1.7 %pad_maximum_fusion = bf16[9,256,256]{2,0,1:T(8,128)(2,1)} fusion(bf16[9,256,128]{2,0,1:T(8,128)(2,1)S(1)} %get-tuple-element.10, bf16[9,256,128]{2,0,1:T(8,128)(2,1)S(1)} %get-tuple-element.9), kind=kLoop, calls=%fused_computation.24 | loop fusion | flops 2359296 | bytes 2359296 | tf_op jit(solution)/shard_map/concatenate | solution.py:62
  55.5 1.7 %fusion.35 = bf16[2,64,2,256]{3,1,0,2:T(8,128)(2,1)S(1)} fusion(bf16[2,2,256,512]{3,2,1,0:T(8,128)(2,1)} %all-gather.2.cloned.1.call-done, s32[64]{0:T(128)S(1)} %dynamic_slice.3), kind=kOutput, calls=%fused_computation.48 | convolution fusion | flops 67207168 | bytes 1179904 | tf_op jit(solution)/shard_map/rkqf,fg->kgrq/dot_general | solution.py:102
  57.2 0.8 copy.60
  58.0 5.0 %all-to-all-start.1 = ((bf16[2,64,2,256]{3,0,2,1:T(2,128)(2,1)}), bf16[2,64,2,256]{3,0,2,1:T(2,128)(2,1)S(1)}, u32[]{:S(2)}, u32[]{:S(2)}) async-start(bf16[2,64,2,256]{3,0,2,1:T(2,128)(2,1)} %copy.60), calls=%async_computation.1 | async-start | bytes 262144 | tf_op jit(solution)/shard_map/all_to_all | solution.py:110
  63.0 5.3 %convolution_bitcast_fusion = f32[9,512,256]{1,2,0:T(8,128)} fusion(bf16[512,256,1]{1,0,2:T(8,128)(2,1)S(1)} %copy-done, bf16[9,256,256]{2,0,1:T(8,128)(2,1)} %pad_maximum_fusion), kind=kOutput, calls=%fused_computation.21 | convolution fusion | flops 603979776 | bytes 6160384 | tf_op jit(solution)/shard_map/qt,ktc->kqc/dot_general | solution.py:63
  68.3 2.1 %all-to-all-done.1 = bf16[2,64,2,256]{3,0,2,1:T(2,128)(2,1)S(1)} async-done(((bf16[2,64,2,256]{3,0,2,1:T(2,128)(2,1)}), bf16[2,64,2,256]{3,0,2,1:T(2,128)(2,1)S(1)}, u32[]{:S(2)}, u32[]{:S(2)}) %all-to-all-start.1) | async-done | bytes 131104 | tf_op jit(solution)/shard_map/all_to_all | solution.py:110
  70.5 0.1 broadcast_in_dim.92
  70.6 0.1 broadcast_in_dim.91
  70.7 3.1 %subtract_convert_fusion.1 = (bf16[9,256,128]{1,2,0:T(8,128)(2,1)S(1)}, bf16[9,256,128]{1,2,0:T(8,128)(2,1)S(1)}) fusion(f32[9,256,128]{1,2,0:T(8,128)S(1)} %bitcast.84, f32[9,256,128]{1,2,0:T(8,128)S(1)} %bitcast.85, f32[9,512,256]{1,2,0:T(8,128)} %convolution_bitcast_fusion), kind=kLoop, calls=%fused_computation.46 | loop fusion | flops 2949120 | bytes 8257536 | tf_op jit(solution)/shard_map/convert_element_type | solution.py:74
  73.8 3.0 %fusion.30 = f32[9,256,512]{2,1,0:T(8,128)} fusion(bf16[512,256,1]{1,0,2:T(8,128)(2,1)S(1)} %copy-done, bf16[9,256,128]{1,2,0:T(8,128)(2,1)S(1)} %get-tuple-element.8, bf16[9,256,128]{1,2,0:T(8,128)(2,1)S(1)} %get-tuple-element.7), kind=kOutput, calls=%fused_computation.40 | convolution fusion | flops 606339072 | bytes 6160384 | tf_op jit(solution)/shard_map/qt,ktc->kqc/dot_general | solution.py:63
  76.8 9.0 %copy.63 = f32[9,256,512]{1,0,2:T(8,128)} copy(f32[9,256,512]{2,1,0:T(8,128)} %fusion.30) | data formatting | bytes 9437184 | tf_op jit(solution)/shard_map/qt,ktc->kqc/dot_general | solution.py:63
  85.8 0.0 copy-start.11
  85.8 5.4 %fusion.13 = f32[256,128,8]{1,2,0:T(8,128)S(1)} fusion(f32[9,8,1]{0,1,2:T(8,128)S(1)} %copy-done.12, f32[9,256]{0,1:T(8,128)S(1)} %copy-done.3, f32[9,256]{0,1:T(8,128)S(1)} %copy-done.5, f32[9,512,256]{2,0,1:T(8,128)} %bitcast.82), kind=kOutput, calls=%fused_computation.25 | convolution fusion | flops 29786112 | bytes 5785888 | tf_op jit(solution)/shard_map/ka,kbc->abc/dot_general | solution.py:83
  91.2 4.9 %fusion.27 = bf16[8,256,128]{2,0,1:T(8,128)(2,1)S(1)} fusion(f32[256,128,8]{1,2,0:T(8,128)S(1)} %fusion.13, f32[9,8,1]{0,1,2:T(8,128)S(1)} %copy-done.11, f32[9,256]{0,1:T(8,128)S(1)} %copy-done.3, f32[9,256]{0,1:T(8,128)S(1)} %copy-done.5, f32[9,512,256]{2,0,1:T(8,128)} %bitcast.83), kind=kOutput, calls=%fused_computation.37 | convolution fusion | flops 30310400 | bytes 6310176 | tf_op jit(solution)/shard_map/ka,kbc->abc/dot_general | solution.py:83
  96.1 0.1 copy.64
  96.2 0.0 copy-start.7
  96.2 18.2 %all_to_all.40 = bf16[8,256,128]{2,1,0:T(8,128)(2,1)} all-to-all(bf16[8,256,128]{2,1,0:T(8,128)(2,1)S(1)} %copy.64), channel_id=1, replica_groups=mesh['ctx'=8,'ch'=4] {'ctx'}, dimensions={0} | all-to-all | bytes 1048576 | tf_op jit(solution)/shard_map/all_to_all | solution.py:114
  114.4 2.0 %copy.65 = bf16[8,256,128]{1,2,0:T(8,128)(2,1)} copy(bf16[8,256,128]{2,1,0:T(8,128)(2,1)} %all_to_all.40) | data formatting | bytes 1048576 | tf_op jit(solution)/shard_map/all_to_all | solution.py:114
  116.5 1.1 bitcast_convert_fusion
  117.6 1.1 fusion.37
  118.7 2.0 %copy.66 = bf16[256,1024]{1,0:T(8,128)(2,1)} copy(bf16[256,1024]{0,1:T(8,128)(2,1)} %fusion.37) | data formatting | bytes 1048576 | tf_op jit(solution)/shard_map/convert_element_type | solution.py:118
  (34 shorter events, 0.2 us)
Async XLA Ops:
  7.3 9.2 %collective-permute-start = (bf16[6,3,1024]{2,0,1:T(8,128)(2,1)S(1)}, bf16[6,3,1024]{2,0,1:T(8,128)(2,1)S(1)}, u32[]{:S(2)}, u32[]{:S(2)}) collective-permute-start(bf16[6,3,1024]{2,0,1:T(8,128)(2,1)S(1)} %slice.99), channel_id=1, source_target_pairs={{0,4},{4,8},{8,12},{12,16},{16,20},{20,24},{24,28},{1,5},{5,9},{9,... | collective-permute-start | bytes 110600 | tf_op jit(solution)/shard_map/ppermute | solution.py:17
  26.4 8.0 %copy-start.9 = (f32[2,2,128]{2,1,0:T(2,128)S(1)}, f32[2,2,128]{2,1,0:T(2,128)}, u32[]{:S(2)}) copy-start(f32[2,2,128]{2,1,0:T(2,128)} %param.18) | copy-start | bytes 6148
  26.4 8.0 %copy-start.1 = (bf16[2,2,256,128]{3,2,1,0:T(8,128)(2,1)S(1)}, bf16[2,2,256,128]{3,2,1,0:T(8,128)(2,1)}, u32[]{:S(2)}) copy-start(bf16[2,2,256,128]{3,2,1,0:T(8,128)(2,1)} %param.17) | copy-start | bytes 786436
  27.3 7.9 %copy-start.10 = (s32[256]{0:T(256)S(1)}, s32[256]{0:T(256)}, u32[]{:S(2)}) copy-start(s32[256]{0:T(256)} %param.19) | copy-start | bytes 3076
  27.3 21.3 %copy-start.6 = (f32[9,8,1]{0,1,2:T(8,128)S(1)}, f32[9,8,1]{0,1,2:T(8,128)}, u32[]{:S(2)}) copy-start(f32[9,8,1]{0,1,2:T(8,128)} %constant.58) | copy-start | bytes 868
  29.4 19.2 %all-to-all-start = ((bf16[256,8,128]{2,0,1:T(8,128)(2,1)}), bf16[256,8,128]{2,0,1:T(8,128)(2,1)}, u32[]{:S(2)}, u32[]{:S(2)}) async-start(bf16[256,8,128]{2,0,1:T(8,128)(2,1)} %copy.57), calls=%async_computation | async-start | bytes 1048576 | tf_op jit(solution)/shard_map/all_to_all | solution.py:107
  34.3 16.5 %copy-start.2 = (f32[9,256]{0,1:T(8,128)S(1)}, f32[9,256]{0,1:T(8,128)}, u32[]{:S(2)}) copy-start(f32[9,256]{0,1:T(8,128)} %constant.52.clone) | copy-start | bytes 27652
  34.3 16.5 %copy-start.8 = (f32[9,8,1]{0,1,2:T(8,128)S(1)}, f32[9,8,1]{0,1,2:T(8,128)}, u32[]{:S(2)}) copy-start(f32[9,8,1]{0,1,2:T(8,128)} %constant.59) | copy-start | bytes 868
  34.3 21.2 %all-gather.2.cloned.1.call-start = ((), (), s32[]{:S(2)}) async-start(), calls=%async_computation.3 | async-start | bytes 1310720 | tf_op jit(solution)/shard_map/all_gather | solution.py:99
  35.2 15.6 %copy-start.4 = (f32[9,256]{0,1:T(8,128)S(1)}, f32[9,256]{0,1:T(8,128)}, u32[]{:S(2)}) copy-start(f32[9,256]{0,1:T(8,128)} %constant.51.clone) | copy-start | bytes 27652
  53.9 9.1 %copy-start = (bf16[512,256,1]{1,0,2:T(8,128)(2,1)S(1)}, bf16[512,256,1]{1,0,2:T(8,128)(2,1)}, u32[]{:S(2)}) copy-start(bf16[512,256,1]{1,0,2:T(8,128)(2,1)} %constant.60) | copy-start | bytes 786436
  58.0 12.4 %all-to-all-start.1 = ((bf16[2,64,2,256]{3,0,2,1:T(2,128)(2,1)}), bf16[2,64,2,256]{3,0,2,1:T(2,128)(2,1)S(1)}, u32[]{:S(2)}, u32[]{:S(2)}) async-start(bf16[2,64,2,256]{3,0,2,1:T(2,128)(2,1)} %copy.60), calls=%async_computation.1 | async-start | bytes 262144 | tf_op jit(solution)/shard_map/all_to_all | solution.py:110
  76.8 9.0 %copy-start.3 = (f32[9,256]{0,1:T(8,128)S(1)}, f32[9,256]{0,1:T(8,128)}, u32[]{:S(2)}) copy-start(f32[9,256]{0,1:T(8,128)} %constant.52.clone) | copy-start | bytes 27652
  76.8 9.0 %copy-start.5 = (f32[9,256]{0,1:T(8,128)S(1)}, f32[9,256]{0,1:T(8,128)}, u32[]{:S(2)}) copy-start(f32[9,256]{0,1:T(8,128)} %constant.51.clone) | copy-start | bytes 27652
  76.8 9.0 %copy-start.12 = (f32[9,8,1]{0,1,2:T(8,128)S(1)}, f32[9,8,1]{0,1,2:T(8,128)}, u32[]{:S(2)}) copy-start(f32[9,8,1]{0,1,2:T(8,128)} %constant.62) | copy-start | bytes 868
  85.8 5.4 %copy-start.11 = (f32[9,8,1]{0,1,2:T(8,128)S(1)}, f32[9,8,1]{0,1,2:T(8,128)}, u32[]{:S(2)}) copy-start(f32[9,8,1]{0,1,2:T(8,128)} %constant.61) | copy-start | bytes 868
  96.2 21.4 %copy-start.7 = (f32[1024]{0:T(1024)S(1)}, f32[1024]{0:T(1024)}, u32[]{:S(2)}) copy-start(f32[1024]{0:T(1024)} %param.16) | copy-start | bytes 12292
Sparse Core Ops, SparseCore 0:
  36.7 18.2 all-gather.1
where the time goes:
time: 129 us; the launch traced here: 128 us
  matrix products  25.5 us (20%)
  local copies, waits for them, and re-layouts  21.6 us (17%)
  other arithmetic  18.4 us (14%)
  blocking collectives  18.2 us (14%)
  waiting for transfers between devices  15.5 us (12%)
  starting transfers between devices  14.7 us (11%)
  between operations  13.8 us (11%)
    all_to_all x1, blocking collectives, per_device(): lax.all_to_all(signal.astype(jnp.bfloat16), 'ctx', split_axis=0, concat_a...  18.2 us
    all_to_all x1, waiting for transfers between devices, per_device(): lax.all_to_all(mixed_in.astype(jnp.bfloat16), 'ctx', split_axis=1, concat...  13.4 us
    dot_general x1, local copies, waits for them, and re-layouts, inner(): out = jnp.einsum('qt,ktc->kqc', table, both, preferred_element_type=f32)  8.99 us
    add x1, other arithmetic, featurize(): featured + jnp.where(same[:, None, None], feat_weight[:, tap_index, :][No...  8.41 us
    dot_general x2, matrix products, inner(): out = jnp.einsum('qt,ktc->kqc', table, both, preferred_element_type=f32)  8.33 us
    dot_general x1, matrix products, long_conv(): jnp.einsum('ka,kbc->abc', back_i, t_imag, precision=high)  5.42 us
    all_to_all x1, starting transfers between devices, per_device(): lax.all_to_all(chosen, 'ctx', split_axis=1, concat_axis=0, tiled=True)  4.96 us
    all_to_all x1, starting transfers between devices, per_device(): lax.all_to_all(mixed_in.astype(jnp.bfloat16), 'ctx', split_axis=1, concat...  4.88 us
  transfers between devices with their start and end apart: 4, of which 2 were waited for; matrix products, arithmetic and copies ran while one was open for 14% of the time, Pallas kernels for 0%

commit v1 on v0

--- a/solution.py
+++ b/solution.py
@@ -1,9 +1,12 @@
+import functools
 import math
 
 import jax
 import jax.numpy as jnp
 import numpy as np
 from jax import lax
+from jax.experimental import pallas as pl
+from jax.experimental.pallas import tpu as pltpu
 from jax.sharding import PartitionSpec as P
 
 GROUP_CH = 16
@@ -85,7 +88,7 @@
     )
 
 
-def per_device(
+def by_collectives(
     streams, feat_weight, skip_gain, spectrum_values, spectrum_scales, group_filter, doc_lengths
 ):
     tokens = streams.shape[0]
@@ -118,6 +121,384 @@
     return (query * (conv + skip_gain[None] * mixed_in)).astype(jnp.bfloat16)
 
 
+LANES = 128
+
+
+def block_kernel(
+    ctx_count, ch_count,
+    streams, inside, taps, gain, values, scales, onehot, spread, dft_hbm, twist_hbm,
+    out,
+    dft, twist, ext, rim, chosen, bank, mine, spec, keep, query, sends, columns,
+    inner_in, inner_out, signal, back,
+    table_sem, rim_sem, ch_send, ch_recv, spec_send, spec_recv, last_send, last_recv,
+    go_send, go_recv, back_send, back_recv,
+):
+    f32, bf16 = jnp.float32, jnp.bfloat16
+    tokens = streams.shape[1]
+    me = lax.axis_index("ctx")
+    my_ch = lax.axis_index("ch")
+    total_len = 2 * tokens * ctx_count
+
+    def remote(src, dst, send, recv, ctx_to, ch_to):
+        return pltpu.make_async_remote_copy(
+            src_ref=src, dst_ref=dst, send_sem=send, recv_sem=recv,
+            device_id=(ctx_to, ch_to), device_id_type=pl.DeviceIdType.MESH,
+        )
+
+    def ctx_at(step):
+        return lax.rem(me + step, ctx_count)
+
+    def ch_at(step):
+        return lax.rem(my_ch + step, ch_count)
+
+    load_dft = pltpu.make_async_copy(dft_hbm, dft, table_sem.at[0])
+    load_twist = pltpu.make_async_copy(twist_hbm, twist, table_sem.at[1])
+    load_dft.start()
+    load_twist.start()
+
+    barrier = pltpu.get_barrier_semaphore()
+    for step in range(1, ctx_count):
+        pl.semaphore_signal(
+            barrier, inc=1, device_id=(ctx_at(step), my_ch), device_id_type=pl.DeviceIdType.MESH
+        )
+    for step in range(1, ch_count):
+        pl.semaphore_signal(
+            barrier, inc=1, device_id=(me, ch_at(step)), device_id_type=pl.DeviceIdType.MESH
+        )
+    pl.semaphore_wait(barrier, ctx_count + ch_count - 2)
+
+    send_rim = remote(
+        streams.at[:, pl.ds(tokens - 16, 16), :], rim, rim_sem.at[0], rim_sem.at[1],
+        ctx_at(1), my_ch,
+    )
+    send_rim.start()
+
+    halves = tokens // SCALE_BLOCK
+    for row in range(2):
+        parts = []
+        for part in range(2):
+            bands = []
+            for half in range(halves):
+                band = values[part, row, half * SCALE_BLOCK : (half + 1) * SCALE_BLOCK, :]
+                bands.append(band.astype(f32) * scales[row, half : half + 1, :])
+            scaled = jnp.concatenate(bands, axis=0).astype(bf16)
+            parts.append(
+                lax.dot_general(
+                    onehot[...], scaled, (((1,), (1,)), ((), ())), preferred_element_type=f32
+                )
+            )
+        for h in range(ch_count):
+            for c in range(ctx_count):
+                at = (h * ctx_count + c) * 8
+                chosen[h, row, c] = jnp.concatenate(
+                    [parts[0][at : at + 8], parts[1][at : at + 8]], axis=0
+                ).astype(bf16)
+
+    def ch_copy(step):
+        to = ch_at(step)
+        return remote(
+            chosen.at[to], bank.at[my_ch], ch_send.at[step], ch_recv.at[step], me, to
+        )
+
+    for step in range(1, ch_count):
+        ch_copy(step).start()
+
+    send_rim.wait()
+    chunk = 64
+
+    def feature(stream, lanes, store):
+        ext[0:8, :] = rim[stream, :, lanes].astype(f32)[8:16]
+        ext[8 : 8 + tokens, :] = streams[stream, :, lanes].astype(f32)
+        for at in range(0, tokens, chunk):
+            where_in = inside[at : at + chunk, :]
+            total = jnp.zeros((chunk, LANES), f32)
+            for tap in range(FEAT_TAPS):
+                index = stream * FEAT_TAPS + tap
+                term = taps[index : index + 1, lanes] * ext[at + 8 - tap : at + 8 - tap + chunk, :]
+                if tap:
+                    term = jnp.where(where_in >= tap, term, 0.0)
+                total = total + term
+            store(at, total)
+
+    def product(block):
+        lanes = pl.ds(pl.multiple_of(block * LANES, LANES), LANES)
+
+        def put_key(at, total):
+            keep[block, at : at + chunk, :] = total
+
+        def put_product(at, total):
+            both = keep[block, at : at + chunk, :] * total
+            keep[block, at : at + chunk, :] = both
+            sends[block, at : at + chunk, :] = both.astype(bf16)
+
+        feature(1, lanes, put_key)
+        feature(2, lanes, put_product)
+
+    def order(index):
+        return 1 + lax.rem(index + 3, ctx_count - 1)
+
+    def go_copy(step):
+        to = ctx_at(step)
+        return remote(sends.at[to], columns.at[me], go_send.at[step], go_recv.at[step], to, my_ch)
+
+    def go(index, carry):
+        step = order(index)
+        product(ctx_at(step))
+        go_copy(step).start()
+        return carry
+
+    lax.fori_loop(0, ctx_count - 1, go, 0)
+    product(me)
+    columns[me] = sends[me]
+
+    for step in range(1, ch_count):
+        ch_copy(step).wait()
+    bank[my_ch] = chosen[my_ch]
+    for row in range(2):
+        for c in range(ctx_count):
+            total = bank[0, row, c].astype(f32)
+            for h in range(1, ch_count):
+                total = total + bank[h, row, c].astype(f32)
+            mine[row, c] = total.astype(bf16)
+
+    def spec_copy(step):
+        to = ctx_at(step)
+        return remote(
+            mine.at[0, to], spec.at[me], spec_send.at[step], spec_recv.at[step], to, my_ch
+        )
+
+    def last_copy(step):
+        return remote(
+            mine.at[1, step], spec.at[ctx_count], last_send.at[step], last_recv.at[0], step, my_ch
+        )
+
+    for step in range(1, ctx_count):
+        spec_copy(step).start()
+    spec[me] = mine[0, me]
+
+    @pl.when(me == 0)
+    def _():
+        for step in range(1, ctx_count):
+            last_copy(step).start()
+        spec[ctx_count] = mine[1, 0]
+
+    def ask(block, carry):
+        lanes = pl.ds(pl.multiple_of(block * LANES, LANES), LANES)
+
+        def put_query(at, total):
+            query[block, at : at + chunk, :] = total
+
+        feature(0, lanes, put_query)
+        return carry
+
+    lax.fori_loop(0, ctx_count, ask, 0)
+
+    load_dft.wait()
+    load_twist.wait()
+    for step in range(1, ctx_count):
+        spec_copy(step).wait()
+
+    @pl.when(me == 0)
+    def _():
+        for step in range(1, ctx_count):
+            last_copy(step).wait_send()
+
+    @pl.when(me != 0)
+    def _():
+        last_copy(1).wait_recv()
+
+    for step in range(1, ctx_count):
+        go_copy(step).wait()
+
+    half = ctx_count // 2
+    rows = 16
+
+    def co(a, k):
+        return math.cos(math.pi * (a * k % (2 * ctx_count)) / ctx_count)
+
+    def si(a, k):
+        return math.sin(math.pi * (a * k % (2 * ctx_count)) / ctx_count)
+
+    def gather(terms, coefs):
+        total = None
+        for term, coef in zip(terms, coefs):
+            if abs(coef) < 1e-9:
+                continue
+            if abs(coef - 1) < 1e-9:
+                piece = term
+            elif abs(coef + 1) < 1e-9:
+                piece = -term
+            else:
+                piece = term * coef
+            total = piece if total is None else total + piece
+        return jnp.zeros_like(terms[0]) if total is None else total
+
+    def outer_step(index, carry):
+        at = pl.ds(pl.multiple_of(index * rows, rows), rows)
+        x = [columns[a, at, :].astype(f32) for a in range(ctx_count)]
+        even, odd = list(range(0, ctx_count, 2)), list(range(1, ctx_count, 2))
+
+        def put(k, real, imag):
+            c, s = twist[k, 0, at, :], twist[k, 1, at, :]
+            inner_in[k, at, 0:LANES] = (real * c + imag * s).astype(bf16)
+            inner_in[k, at, LANES : 2 * LANES] = (imag * c - real * s).astype(bf16)
+
+        for k in range(half + 1):
+            ce = gather([x[a] for a in even], [co(a, k) for a in even])
+            cd = gather([x[a] for a in odd], [co(a, k) for a in odd])
+            se = gather([x[a] for a in even], [si(a, k) for a in even])
+            sd = gather([x[a] for a in odd], [si(a, k) for a in odd])
+            put(k, ce + cd, -(se + sd))
+            if k != ctx_count - k:
+                put(ctx_count - k, ce - cd, se - sd)
+        return carry
+
+    lax.fori_loop(0, tokens // rows, outer_step, 0)
+
+    def inner(both):
+        result = jnp.dot(dft[...], both, preferred_element_type=f32)
+        return (
+            result[:tokens, :LANES], result[:tokens, LANES:],
+            result[tokens:, :LANES], result[tokens:, LANES:],
+        )
+
+    def row_step(k, carry):
+        picked = spec[k].astype(f32).T.astype(bf16)
+        wide = jnp.dot(picked, spread[...], preferred_element_type=f32)
+        s_real, s_imag = wide[:, :LANES], wide[:, LANES:]
+        cr, ci, sr, sj = inner(inner_in[k])
+        z_real, z_imag = cr + sj, ci - sr
+        p_real = (z_real * s_real - z_imag * s_imag).astype(bf16)
+        p_imag = (z_real * s_imag + z_imag * s_real).astype(bf16)
+        cr, ci, sr, sj = inner(jnp.concatenate([p_real, p_imag], axis=1))
+        v_real, v_imag = cr - sj, ci + sr
+        c, s = twist[k, 0], twist[k, 1]
+        inner_out[k, 0] = v_real * c - v_imag * s
+        inner_out[k, 1] = v_imag * c + v_real * s
+        return carry
+
+    lax.fori_loop(0, ctx_count + 1, row_step, 0)
+
+    def last_step(index, carry):
+        at = pl.ds(pl.multiple_of(index * rows, rows), rows)
+        real = [inner_out[k, 0, at, :] for k in range(ctx_count + 1)]
+        imag = [inner_out[k, 1, at, :] for k in range(ctx_count + 1)]
+        for parity in range(2):
+            sign = 1.0 if parity == 0 else -1.0
+            folded_r = [real[k] + sign * real[ctx_count - k] for k in range(half)] + [real[half]]
+            folded_i = [imag[k] - sign * imag[ctx_count - k] for k in range(half)] + [imag[half]]
+            for a in range(parity, ctx_count, 2):
+                weights = [(1.0 if k == 0 else 2.0) for k in range(half + 1)]
+                total = gather(
+                    folded_r + folded_i,
+                    [w * co(a, k) for k, w in enumerate(weights)]
+                    + [-w * si(a, k) for k, w in enumerate(weights)],
+                )
+                signal[a, at, :] = (total * (1.0 / total_len)).astype(bf16)
+        return carry
+
+    lax.fori_loop(0, tokens // rows, last_step, 0)
+
+    def back_copy(step):
+        to = ctx_at(step)
+        return remote(signal.at[to], back.at[me], back_send.at[step], back_recv.at[step], to, my_ch)
+
+    def send_back(index, carry):
+        back_copy(order(index)).start()
+        return carry
+
+    lax.fori_loop(0, ctx_count - 1, send_back, 0)
+
+    def finish(block, conv):
+        lanes = pl.ds(pl.multiple_of(block * LANES, LANES), LANES)
+        skipped = gain[0:1, lanes] * keep[block]
+        out[:, lanes] = (query[block] * (conv.astype(f32) + skipped)).astype(bf16)
+
+    finish(me, signal[me])
+
+    def receive(index, carry):
+        step = order(index)
+        back_copy(step).wait()
+        source = lax.rem(me + ctx_count - step, ctx_count)
+        finish(source, back[source])
+        return carry
+
+    lax.fori_loop(0, ctx_count - 1, receive, 0)
+
+
+def fused(streams, inside, feat_weight, skip_gain, spectrum_values, spectrum_scales, onehot):
+    ctx_count, ch_count = lax.axis_size("ctx"), lax.axis_size("ch")
+    tokens, _, local_ch = streams.shape
+    rows = ctx_count + 1
+    f32, bf16 = jnp.float32, jnp.bfloat16
+    cos_t, sin_t = wave(np.arange(rows), np.arange(tokens), 2 * tokens * ctx_count)
+    twist = np.stack([cos_t, sin_t], axis=1).astype(np.float32)[..., None]
+    twist = np.ascontiguousarray(np.broadcast_to(twist, twist.shape[:3] + (LANES,)))
+    cos_i, sin_i = wave(np.arange(tokens), np.arange(tokens), tokens)
+    dft = jnp.asarray(np.concatenate([cos_i, sin_i], axis=0), bf16)
+    owner = np.arange(2 * LANES) % LANES // GROUP_CH + 8 * (np.arange(2 * LANES) // LANES)
+    spread = jnp.asarray(np.arange(16)[:, None] == owner[None, :], bf16)
+    vmem = pl.BlockSpec(memory_space=pltpu.VMEM)
+    hbm = pl.BlockSpec(memory_space=pl.ANY)
+    dma = lambda count: pltpu.SemaphoreType.DMA((count,))
+    block = (ctx_count, tokens, LANES)
+    picks = (2, ctx_count, 16, tokens)
+    return pl.pallas_call(
+        functools.partial(block_kernel, ctx_count, ch_count),
+        out_shape=jax.ShapeDtypeStruct((tokens, local_ch), bf16),
+        in_specs=[vmem] * 8 + [hbm] * 2,
+        out_specs=vmem,
+        scratch_shapes=[
+            pltpu.VMEM((2 * tokens, tokens), bf16),
+            pltpu.VMEM((rows, 2, tokens, LANES), f32),
+            pltpu.VMEM((tokens + 8, LANES), f32),
+            pltpu.VMEM((3, 16, local_ch), bf16),
+            pltpu.VMEM((ch_count,) + picks, bf16),
+            pltpu.VMEM((ch_count,) + picks, bf16),
+            pltpu.VMEM(picks, bf16),
+            pltpu.VMEM((rows, 16, tokens), bf16),
+            pltpu.VMEM(block, f32),
+            pltpu.VMEM(block, f32),
+            pltpu.VMEM(block, bf16),
+            pltpu.VMEM(block, bf16),
+            pltpu.VMEM((rows, tokens, 2 * LANES), bf16),
+            pltpu.VMEM((rows, 2, tokens, LANES), f32),
+            pltpu.VMEM(block, bf16),
+            pltpu.VMEM(block, bf16),
+            dma(2), dma(2), dma(ch_count), dma(ch_count), dma(ctx_count), dma(ctx_count),
+            dma(ctx_count), dma(1), dma(ctx_count), dma(ctx_count), dma(ctx_count), dma(ctx_count),
+        ],
+        compiler_params=pltpu.CompilerParams(
+            collective_id=0, has_side_effects=True, vmem_limit_bytes=40 * 2**20
+        ),
+    )(
+        jnp.transpose(streams, (1, 0, 2)), inside, feat_weight.reshape(-1, local_ch),
+        skip_gain[None], spectrum_values, spectrum_scales, onehot, spread, dft,
+        jnp.asarray(twist),
+    )
+
+
+def per_device(
+    streams, feat_weight, skip_gain, spectrum_values, spectrum_scales, group_filter, doc_lengths
+):
+    tokens, _, local_ch = streams.shape
+    filters = spectrum_values.shape[3]
+    if local_ch != lax.axis_size("ctx") * LANES or filters % LANES or tokens % SCALE_BLOCK:
+        return by_collectives(
+            streams, feat_weight, skip_gain, spectrum_values, spectrum_scales, group_filter,
+            doc_lengths,
+        )
+    positions = lax.axis_index("ctx") * tokens + jnp.arange(tokens, dtype=jnp.int32)
+    ends = jnp.cumsum(doc_lengths)
+    begins = jnp.max(jnp.where(positions[:, None] >= ends[None, :], ends[None, :], 0), axis=1)
+    inside = jnp.broadcast_to((positions - begins)[:, None], (tokens, LANES))
+    held = lax.axis_index("ch") * filters + jnp.arange(filters, dtype=jnp.int32)
+    onehot = (group_filter[:, None] == held[None, :]).astype(jnp.bfloat16)
+    return fused(
+        streams, inside, feat_weight, skip_gain, spectrum_values, spectrum_scales, onehot
+    )
+
+
 def solution(mesh):
     placed = (
         P("ctx", None, "ch"),

time: 129 us -> 55.5 us (0.43)
  Pallas kernels: 0 us -> 44.4 us
  matrix products: 25.5 us -> 0 us
  blocking collectives: 18.2 us -> 0 us
  other arithmetic: 18.4 us -> 1.05 us
  waiting for transfers between devices: 15.5 us -> 0 us
  starting transfers between devices: 14.7 us -> 0 us
  between operations: 13.8 us -> 0.05 us
  local copies, waits for them, and re-layouts: 21.6 us -> 9.56 us
    pallas_call x0 -> x1, Pallas kernels: none -> 44.4 us  [fused(): pl.pallas_call(functools.partial(block_kernel, ctx_count, ch_count), out_...]
    dot_general x7 -> x0, matrix products: 25.5 us -> none  [the longest x2 8.33 us: inner(): out = jnp.einsum('qt,ktc->kqc', table, both, preferred_element_type=f32)]
    all_to_all x1 -> x0, blocking collectives: 18.2 us -> none  [per_device(): lax.all_to_all(signal.astype(jnp.bfloat16), 'ctx', split_axis=0, concat_a...]
    all_to_all x2 -> x0, waiting for transfers between devices: 15.5 us -> none  [the longest x1 13.4 us: per_device(): lax.all_to_all(mixed_in.astype(jnp.bfloat16), 'ctx', split_axis=1, concat...]
    all_to_all x2 -> x0, starting transfers between devices: 9.84 us -> none  [the longest x1 4.96 us: per_device(): lax.all_to_all(chosen, 'ctx', split_axis=1, concat_axis=0, tiled=True)]
    dot_general x1 -> x0, local copies, waits for them, and re-layouts: 8.99 us -> none  [inner(): out = jnp.einsum('qt,ktc->kqc', table, both, preferred_element_type=f32)]
    add x2, other arithmetic: 8.41 us -> 0.01 us  [the longest x1 0.01 us: per_device(): held = lax.axis_index('ch') * filters + jnp.arange(filters, dtype=jnp.int32)]
    convert_element_type x7 -> x1, other arithmetic: 7.98 us -> 0.78 us  [per_device(): onehot = (group_filter[:, None] == held[None, :]).astype(jnp.bfloat16)]
  transfers between devices with their start and end apart: 4 -> 0, of which waited for: 2 -> 0; matrix products, arithmetic and copies ran while one was open for 14% -> 0% of each run, Pallas kernels for 0% -> 0%
where the time goes in v1:
time: 55.5 us; the launch traced here: 55.1 us
  Pallas kernels  44.4 us (80%)
  local copies, waits for them, and re-layouts  9.56 us (17%)
  other arithmetic  1.05 us (2%)
    pallas_call x1, Pallas kernels, fused(): pl.pallas_call(functools.partial(block_kernel, ctx_count, ch_count), out_...  44.4 us
    unnamed x15, local copies, waits for them, and re-layouts  7.83 us

profile of v1, /device:TPU:0, one launch (start us, length us, event | category | flops | bytes accessed | tf_op | source)
XLA Modules:
  0.0 55.1 jit_solution(9549689382336511516)
XLA Ops:
  0.0 0.7 %copy.13 = s32[32,1]{1,0:T(8,128)S(1)} copy(s32[32,1]{0,1:T(1,128)} %bitcast.5) | data formatting | bytes 256 | tf_op jit(solution)/shard_map/reshape.31
  0.7 0.1 reduce-window.8
  0.8 0.1 reduce
  0.9 0.1 select_reduce_fusion
  1.0 0.8 %compare_convert_fusion.onehot = bf16[256,128]{1,0:T(8,128)(2,1)S(1)} fusion(s32[128]{0:T(128)S(1)} %iota_add_fusion.1, s32[256]{0:T(256)} %param.15), kind=kLoop, calls=%fused_computation | loop fusion | flops 65536 | bytes 67072 | tf_op jit(solution)/shard_map/convert_element_type | solution.py:496
  1.8 0.9 %reshape.43.taps = f32[21,1024]{1,0:T(8,128)S(1)} reshape(f32[3,7,1024]{2,1,0:T(8,128)} %param.11) | data formatting | bytes 172032 | tf_op jit(solution)/shard_map/reshape | solution.py:475
  2.7 0.1 broadcast_in_dim.15.inside
  2.8 0.0 copy-start
  2.8 1.7 %copy-done = f32[9,2,256,128]{3,2,1,0:T(8,128)S(1)} copy-done((f32[9,2,256,128]{3,2,1,0:T(8,128)S(1)}, f32[9,2,256,128]{3,2,1,0:T(8,128)}, u32[]{:S(2)}) %copy-start) | copy-done | bytes 2359320
  4.5 0.0 copy-start.1
  4.5 1.4 %copy-done.1 = bf16[256,3,1024]{2,0,1:T(8,128)(2,1)S(1)} copy-done((bf16[256,3,1024]{2,0,1:T(8,128)(2,1)S(1)}, bf16[256,3,1024]{2,0,1:T(8,128)(2,1)}, u32[]{:S(2)}) %copy-start.1) | copy-done | bytes 1572888
  5.9 0.0 copy-start.2
  5.9 0.9 %copy-done.2 = bf16[2,2,256,128]{3,2,1,0:T(8,128)(2,1)S(1)} copy-done((bf16[2,2,256,128]{3,2,1,0:T(8,128)(2,1)S(1)}, bf16[2,2,256,128]{3,2,1,0:T(8,128)(2,1)}, u32[]{:S(2)}) %copy-start.2) | copy-done | bytes 262168
  6.8 0.0 copy-start.3
  6.8 0.9 %copy-done.3 = bf16[512,256]{1,0:T(8,128)(2,1)S(1)} copy-done((bf16[512,256]{1,0:T(8,128)(2,1)S(1)}, bf16[512,256]{1,0:T(8,128)(2,1)}, u32[]{:S(2)}) %copy-start.3) | copy-done | bytes 262168
  7.8 0.0 copy-start.4
  7.8 0.7 %copy-done.4 = bf16[16,256]{1,0:T(8,128)(2,1)S(1)} copy-done((bf16[16,256]{1,0:T(8,128)(2,1)S(1)}, bf16[16,256]{1,0:T(8,128)(2,1)}, u32[]{:S(2)}) %copy-start.4) | copy-done | bytes 8216
  8.5 0.0 copy-start.5
  8.5 0.7 %copy-done.5 = f32[1024]{0:T(1024)S(1)} copy-done((f32[1024]{0:T(1024)S(1)}, f32[1024]{0:T(1024)}, u32[]{:S(2)}) %copy-start.5) | copy-done | bytes 4120
  9.2 0.0 copy-start.6
  9.2 0.7 %copy-done.6 = f32[2,2,128]{2,1,0:T(2,128)S(1)} copy-done((f32[2,2,128]{2,1,0:T(2,128)S(1)}, f32[2,2,128]{2,1,0:T(2,128)}, u32[]{:S(2)}) %copy-start.6) | copy-done | bytes 2072
  9.9 44.4 %shard_map.100 = bf16[256,1024]{1,0:T(8,128)(2,1)S(1)} custom-call(bf16[3,256,1024]{2,1,0:T(8,128)(2,1)S(1)} %bitcast.3, s32[256,128]{1,0:T(8,128)S(1)} %broadcast_in_dim.15.inside, f32[21,1024]{1,0:T(8,128)S(1)} %reshape.43.taps, f32[1,1024]{1,0:T(1,128)S(1)} %bitcast.4, bf16[2,2,256,128]{3,2,1,0:T(8,128)(2,1)S(1)} %copy-done.2, ...), custom_call_target="tpu_custom_call" | custom-call | tf_op jit(solution)/shard_map/pallas_call | solution.py:446
  54.3 0.8 %copy.15 = bf16[256,1024]{1,0:T(8,128)(2,1)} copy(bf16[256,1024]{1,0:T(8,128)(2,1)S(1)} %shard_map.100) | data formatting | bytes 1048576
  (3 shorter events, 0.0 us)
Async XLA Ops:
  2.8 1.7 %copy-start = (f32[9,2,256,128]{3,2,1,0:T(8,128)S(1)}, f32[9,2,256,128]{3,2,1,0:T(8,128)}, u32[]{:S(2)}) copy-start(f32[9,2,256,128]{3,2,1,0:T(8,128)} %constant.28.clone.twist_hbm) | copy-start | bytes 7077892
  4.5 1.4 %copy-start.1 = (bf16[256,3,1024]{2,0,1:T(8,128)(2,1)S(1)}, bf16[256,3,1024]{2,0,1:T(8,128)(2,1)}, u32[]{:S(2)}) copy-start(bf16[256,3,1024]{2,0,1:T(8,128)(2,1)} %param.10) | copy-start | bytes 4718596
  5.9 0.9 %copy-start.2 = (bf16[2,2,256,128]{3,2,1,0:T(8,128)(2,1)S(1)}, bf16[2,2,256,128]{3,2,1,0:T(8,128)(2,1)}, u32[]{:S(2)}) copy-start(bf16[2,2,256,128]{3,2,1,0:T(8,128)(2,1)} %values.1) | copy-start | bytes 786436
  6.8 0.9 %copy-start.3 = (bf16[512,256]{1,0:T(8,128)(2,1)S(1)}, bf16[512,256]{1,0:T(8,128)(2,1)}, u32[]{:S(2)}) copy-start(bf16[512,256]{1,0:T(8,128)(2,1)} %constant.26.clone.dft_hbm) | copy-start | bytes 786436
  7.8 0.7 %copy-start.4 = (bf16[16,256]{1,0:T(8,128)(2,1)S(1)}, bf16[16,256]{1,0:T(8,128)(2,1)}, u32[]{:S(2)}) copy-start(bf16[16,256]{1,0:T(8,128)(2,1)} %constant.27.clone.spread) | copy-start | bytes 24580
  8.5 0.7 %copy-start.5 = (f32[1024]{0:T(1024)S(1)}, f32[1024]{0:T(1024)}, u32[]{:S(2)}) copy-start(f32[1024]{0:T(1024)} %param.12) | copy-start | bytes 12292
  9.2 0.7 %copy-start.6 = (f32[2,2,128]{2,1,0:T(2,128)S(1)}, f32[2,2,128]{2,1,0:T(2,128)}, u32[]{:S(2)}) copy-start(f32[2,2,128]{2,1,0:T(2,128)} %scales.1) | copy-start | bytes 6148

commit v2 on v1

--- a/solution.py
+++ b/solution.py
@@ -126,15 +126,16 @@
 
 def block_kernel(
     ctx_count, ch_count,
-    streams, inside, taps, gain, values, scales, onehot, spread, dft_hbm, twist_hbm,
+    streams_hbm, lengths, taps_hbm, gain_hbm, values_hbm, scales_hbm, groups_hbm, dft_hbm,
+    twist_hbm,
     out,
-    dft, twist, ext, rim, chosen, bank, mine, spec, keep, query, sends, columns,
+    streams, inside, taps, gain, values, scales, groups, dft_wide, dft, twist, wide, ext, rim, chosen, bank, mine, spec, keep, query, sends, columns,
     inner_in, inner_out, signal, back,
     table_sem, rim_sem, ch_send, ch_recv, spec_send, spec_recv, last_send, last_recv,
     go_send, go_recv, back_send, back_recv,
 ):
     f32, bf16 = jnp.float32, jnp.bfloat16
-    tokens = streams.shape[1]
+    tokens = streams_hbm.shape[1]
     me = lax.axis_index("ctx")
     my_ch = lax.axis_index("ch")
     total_len = 2 * tokens * ctx_count
@@ -151,10 +152,18 @@
     def ch_at(step):
         return lax.rem(my_ch + step, ch_count)
 
-    load_dft = pltpu.make_async_copy(dft_hbm, dft, table_sem.at[0])
-    load_twist = pltpu.make_async_copy(twist_hbm, twist, table_sem.at[1])
-    load_dft.start()
-    load_twist.start()
+    loads = [
+        pltpu.make_async_copy(source, target, table_sem.at[index])
+        for index, (source, target) in enumerate(
+            [
+                (values_hbm, values), (scales_hbm, scales), (groups_hbm, groups),
+                (taps_hbm, taps), (streams_hbm, streams),
+                (gain_hbm, gain), (dft_hbm, dft_wide), (twist_hbm, twist),
+            ]
+        )
+    ]
+    for load in loads:
+        load.start()
 
     barrier = pltpu.get_barrier_semaphore()
     for step in range(1, ctx_count):
@@ -165,14 +174,12 @@
         pl.semaphore_signal(
             barrier, inc=1, device_id=(me, ch_at(step)), device_id_type=pl.DeviceIdType.MESH
         )
-    pl.semaphore_wait(barrier, ctx_count + ch_count - 2)
-
-    send_rim = remote(
-        streams.at[:, pl.ds(tokens - 16, 16), :], rim, rim_sem.at[0], rim_sem.at[1],
-        ctx_at(1), my_ch,
-    )
-    send_rim.start()
-
+
+    for load in loads[:3]:
+        load.wait()
+    filters = values.shape[3]
+    held = my_ch * filters + lax.broadcasted_iota(jnp.int32, (filters, groups.shape[1]), 0)
+    onehot = jnp.where(held == groups[...], 1.0, 0.0).astype(f32).T.astype(bf16)
     halves = tokens // SCALE_BLOCK
     for row in range(2):
         parts = []
@@ -184,7 +191,7 @@
             scaled = jnp.concatenate(bands, axis=0).astype(bf16)
             parts.append(
                 lax.dot_general(
-                    onehot[...], scaled, (((1,), (1,)), ((), ())), preferred_element_type=f32
+                    onehot, scaled, (((1,), (1,)), ((), ())), preferred_element_type=f32
                 )
             )
         for h in range(ch_count):
@@ -194,15 +201,45 @@
                     [parts[0][at : at + 8], parts[1][at : at + 8]], axis=0
                 ).astype(bf16)
 
+    begins = jnp.zeros((tokens, LANES), jnp.int32)
+    places = me * tokens + lax.broadcasted_iota(jnp.int32, (tokens, LANES), 0)
+    end = jnp.int32(0)
+    for doc in range(lengths.shape[0]):
+        end = end + lengths[doc]
+        begins = jnp.where(places >= end, end, begins)
+    inside[...] = places - begins
+
+    pl.semaphore_wait(barrier, ctx_count + ch_count - 2)
+
+    send_rim = remote(
+        streams_hbm.at[:, pl.ds(tokens - 16, 16), :], rim, rim_sem.at[0], rim_sem.at[1],
+        ctx_at(1), my_ch,
+    )
+    send_rim.start()
+
     def ch_copy(step):
         to = ch_at(step)
         return remote(
-            chosen.at[to], bank.at[my_ch], ch_send.at[step], ch_recv.at[step], me, to
+            chosen.at[to, 0], bank.at[my_ch, 0], ch_send.at[step], ch_recv.at[step], me, to
+        )
+
+    def ch_extra(step):
+        to = ch_at(step)
+        at = ch_count + step
+        return remote(
+            chosen.at[to, 1], bank.at[my_ch, 1], ch_send.at[at], ch_recv.at[at], me, to
         )
 
     for step in range(1, ch_count):
         ch_copy(step).start()
 
+    @pl.when(me == 0)
+    def _():
+        for step in range(1, ch_count):
+            ch_extra(step).start()
+
+    for load in loads[3:5]:
+        load.wait()
     send_rim.wait()
     chunk = 64
 
@@ -213,8 +250,7 @@
             where_in = inside[at : at + chunk, :]
             total = jnp.zeros((chunk, LANES), f32)
             for tap in range(FEAT_TAPS):
-                index = stream * FEAT_TAPS + tap
-                term = taps[index : index + 1, lanes] * ext[at + 8 - tap : at + 8 - tap + chunk, :]
+                term = taps[stream, tap : tap + 1, lanes] * ext[at + 8 - tap : at + 8 - tap + chunk, :]
                 if tap:
                     term = jnp.where(where_in >= tap, term, 0.0)
                 total = total + term
@@ -253,14 +289,17 @@
 
     for step in range(1, ch_count):
         ch_copy(step).wait()
-    bank[my_ch] = chosen[my_ch]
-    for row in range(2):
+
+    def add_picks(row):
+        bank[my_ch, row] = chosen[my_ch, row]
         for c in range(ctx_count):
             total = bank[0, row, c].astype(f32)
             for h in range(1, ch_count):
                 total = total + bank[h, row, c].astype(f32)
             mine[row, c] = total.astype(bf16)
 
+    add_picks(0)
+
     def spec_copy(step):
         to = ctx_at(step)
         return remote(
@@ -278,6 +317,9 @@
 
     @pl.when(me == 0)
     def _():
+        for step in range(1, ch_count):
+            ch_extra(step).wait()
+        add_picks(1)
         for step in range(1, ctx_count):
             last_copy(step).start()
         spec[ctx_count] = mine[1, 0]
@@ -293,8 +335,8 @@
 
     lax.fori_loop(0, ctx_count, ask, 0)
 
-    load_dft.wait()
-    load_twist.wait()
+    for load in loads[5:]:
+        load.wait()
     for step in range(1, ctx_count):
         spec_copy(step).wait()
 
@@ -306,6 +348,19 @@
     @pl.when(me != 0)
     def _():
         last_copy(1).wait_recv()
+
+    lane = lax.broadcasted_iota(jnp.int32, (16, 2 * LANES), 1)
+    owner = lane % LANES // GROUP_CH + lane // LANES * 8
+    picking = lax.broadcasted_iota(jnp.int32, (16, 2 * LANES), 0) == owner
+    spread = jnp.where(picking, 1.0, 0.0).astype(bf16)
+    dft[...] = dft_wide[...].astype(bf16)
+
+    def widen(k, carry):
+        picked = spec[k].astype(f32).T.astype(bf16)
+        wide[k] = jnp.dot(picked, spread, preferred_element_type=f32)
+        return carry
+
+    lax.fori_loop(0, ctx_count + 1, widen, 0)
 
     for step in range(1, ctx_count):
         go_copy(step).wait()
@@ -362,22 +417,19 @@
             result[tokens:, :LANES], result[tokens:, LANES:],
         )
 
-    def row_step(k, carry):
-        picked = spec[k].astype(f32).T.astype(bf16)
-        wide = jnp.dot(picked, spread[...], preferred_element_type=f32)
-        s_real, s_imag = wide[:, :LANES], wide[:, LANES:]
+    for k in range(ctx_count + 1):
+        s_real, s_imag = wide[k, :, :LANES], wide[k, :, LANES:]
         cr, ci, sr, sj = inner(inner_in[k])
         z_real, z_imag = cr + sj, ci - sr
-        p_real = (z_real * s_real - z_imag * s_imag).astype(bf16)
-        p_imag = (z_real * s_imag + z_imag * s_real).astype(bf16)
-        cr, ci, sr, sj = inner(jnp.concatenate([p_real, p_imag], axis=1))
+        inner_in[k, :, :LANES] = (z_real * s_real - z_imag * s_imag).astype(bf16)
+        inner_in[k, :, LANES:] = (z_real * s_imag + z_imag * s_real).astype(bf16)
+
+    for k in range(ctx_count + 1):
+        cr, ci, sr, sj = inner(inner_in[k])
         v_real, v_imag = cr - sj, ci + sr
         c, s = twist[k, 0], twist[k, 1]
         inner_out[k, 0] = v_real * c - v_imag * s
         inner_out[k, 1] = v_imag * c + v_real * s
-        return carry
-
-    lax.fori_loop(0, ctx_count + 1, row_step, 0)
 
     def last_step(index, carry):
         at = pl.ds(pl.multiple_of(index * rows, rows), rows)
@@ -426,7 +478,10 @@
     lax.fori_loop(0, ctx_count - 1, receive, 0)
 
 
-def fused(streams, inside, feat_weight, skip_gain, spectrum_values, spectrum_scales, onehot):
+def fused(
+    streams, feat_weight, skip_gain, spectrum_values, spectrum_scales, group_filter,
+    doc_lengths
+):
     ctx_count, ch_count = lax.axis_size("ctx"), lax.axis_size("ch")
     tokens, _, local_ch = streams.shape
     rows = ctx_count + 1
@@ -435,9 +490,7 @@
     twist = np.stack([cos_t, sin_t], axis=1).astype(np.float32)[..., None]
     twist = np.ascontiguousarray(np.broadcast_to(twist, twist.shape[:3] + (LANES,)))
     cos_i, sin_i = wave(np.arange(tokens), np.arange(tokens), tokens)
-    dft = jnp.asarray(np.concatenate([cos_i, sin_i], axis=0), bf16)
-    owner = np.arange(2 * LANES) % LANES // GROUP_CH + 8 * (np.arange(2 * LANES) // LANES)
-    spread = jnp.asarray(np.arange(16)[:, None] == owner[None, :], bf16)
+    dft = jnp.asarray(np.concatenate([cos_i, sin_i], axis=0), f32)
     vmem = pl.BlockSpec(memory_space=pltpu.VMEM)
     hbm = pl.BlockSpec(memory_space=pl.ANY)
     dma = lambda count: pltpu.SemaphoreType.DMA((count,))
@@ -446,11 +499,20 @@
     return pl.pallas_call(
         functools.partial(block_kernel, ctx_count, ch_count),
         out_shape=jax.ShapeDtypeStruct((tokens, local_ch), bf16),
-        in_specs=[vmem] * 8 + [hbm] * 2,
+        in_specs=[hbm, pl.BlockSpec(memory_space=pltpu.SMEM)] + [hbm] * 7,
         out_specs=vmem,
         scratch_shapes=[
+            pltpu.VMEM((3, tokens, local_ch), bf16),
+            pltpu.VMEM((tokens, LANES), jnp.int32),
+            pltpu.VMEM(feat_weight.shape, f32),
+            pltpu.VMEM((1, local_ch), f32),
+            pltpu.VMEM(spectrum_values.shape, bf16),
+            pltpu.VMEM(spectrum_scales.shape, f32),
+            pltpu.VMEM((1,) + group_filter.shape, jnp.int32),
+            pltpu.VMEM((2 * tokens, tokens), f32),
             pltpu.VMEM((2 * tokens, tokens), bf16),
             pltpu.VMEM((rows, 2, tokens, LANES), f32),
+            pltpu.VMEM((rows, tokens, 2 * LANES), f32),
             pltpu.VMEM((tokens + 8, LANES), f32),
             pltpu.VMEM((3, 16, local_ch), bf16),
             pltpu.VMEM((ch_count,) + picks, bf16),
@@ -465,16 +527,15 @@
             pltpu.VMEM((rows, 2, tokens, LANES), f32),
             pltpu.VMEM(block, bf16),
             pltpu.VMEM(block, bf16),
-            dma(2), dma(2), dma(ch_count), dma(ch_count), dma(ctx_count), dma(ctx_count),
+            dma(8), dma(2), dma(2 * ch_count), dma(2 * ch_count), dma(ctx_count), dma(ctx_count),
             dma(ctx_count), dma(1), dma(ctx_count), dma(ctx_count), dma(ctx_count), dma(ctx_count),
         ],
         compiler_params=pltpu.CompilerParams(
-            collective_id=0, has_side_effects=True, vmem_limit_bytes=40 * 2**20
+            collective_id=0, has_side_effects=True, vmem_limit_bytes=56 * 2**20
         ),
     )(
-        jnp.transpose(streams, (1, 0, 2)), inside, feat_weight.reshape(-1, local_ch),
-        skip_gain[None], spectrum_values, spectrum_scales, onehot, spread, dft,
-        jnp.asarray(twist),
+        jnp.transpose(streams, (1, 0, 2)), doc_lengths, feat_weight, skip_gain[None],
+        spectrum_values, spectrum_scales, group_filter[None], dft, jnp.asarray(twist),
     )
 
 
@@ -488,14 +549,8 @@
             streams, feat_weight, skip_gain, spectrum_values, spectrum_scales, group_filter,
             doc_lengths,
         )
-    positions = lax.axis_index("ctx") * tokens + jnp.arange(tokens, dtype=jnp.int32)
-    ends = jnp.cumsum(doc_lengths)
-    begins = jnp.max(jnp.where(positions[:, None] >= ends[None, :], ends[None, :], 0), axis=1)
-    inside = jnp.broadcast_to((positions - begins)[:, None], (tokens, LANES))
-    held = lax.axis_index("ch") * filters + jnp.arange(filters, dtype=jnp.int32)
-    onehot = (group_filter[:, None] == held[None, :]).astype(jnp.bfloat16)
     return fused(
-        streams, inside, feat_weight, skip_gain, spectrum_values, spectrum_scales, onehot
+        streams, feat_weight, skip_gain, spectrum_values, spectrum_scales, group_filter, doc_lengths
     )
 
 

time: 55.5 us -> 45.9 us (0.83)
  local copies, waits for them, and re-layouts: 9.56 us -> 1.87 us
  other arithmetic: 1.05 us -> 0 us
    unnamed x15 -> x1, local copies, waits for them, and re-layouts: 7.83 us -> 1.87 us
    reshape x1 -> x0, local copies, waits for them, and re-layouts: 0.91 us -> none  [fused(): feat_weight.reshape(-1, local_ch)]
    convert_element_type x1 -> x0, other arithmetic: 0.78 us -> none  [per_device(): onehot = (group_filter[:, None] == held[None, :]).astype(jnp.bfloat16)]
    another operation x1 -> x0, local copies, waits for them, and re-layouts: 0.74 us -> none
where the time goes in v2:
time: 45.9 us; the launch traced here: 45.8 us
  Pallas kernels  43.9 us (96%)
  local copies, waits for them, and re-layouts  1.87 us (4%)
    pallas_call x1, Pallas kernels, fused(): pl.pallas_call(functools.partial(block_kernel, ctx_count, ch_count), out_...  43.9 us
    unnamed x1, local copies, waits for them, and re-layouts  1.87 us

profile of v2, /device:TPU:0, one launch (start us, length us, event | category | flops | bytes accessed | tf_op | source)
XLA Modules:
  0.0 45.8 jit_solution(9769588901260912645)
XLA Ops:
  0.0 43.9 %shard_map.91 = bf16[256,1024]{1,0:T(8,128)(2,1)} custom-call(bf16[3,256,1024]{2,1,0:T(8,128)(2,1)} %bitcast.3, s32[32]{0:T(128)} %lengths.1, f32[3,7,1024]{2,1,0:T(8,128)} %taps_hbm.1, f32[1,1024]{1,0:T(1,128)} %bitcast.4, bf16[2,2,256,128]{3,2,1,0:T(8,128)(2,1)} %values_hbm.1, f32[2,2,128]{2,1,0:T(2,128)} %scales_hbm.1, s32[1,256]{1,0:T(1,128)} %bitcast.5, ...), custom_call_target="tpu_custom_call" | custom-call | tf_op jit(solution)/shard_map/pallas_call | solution.py:499
  43.9 1.9 %copy.11 = bf16[256,1024]{1,0:T(8,128)(2,1)} copy(bf16[256,1024]{1,0:T(8,128)(2,1)} %shard_map.91) | data formatting | bytes 1048576

commit v3 on v2

--- a/solution.py
+++ b/solution.py
@@ -175,6 +175,22 @@
             barrier, inc=1, device_id=(me, ch_at(step)), device_id_type=pl.DeviceIdType.MESH
         )
 
+    begins = jnp.zeros((tokens, LANES), jnp.int32)
+    places = me * tokens + lax.broadcasted_iota(jnp.int32, (tokens, LANES), 0)
+    end = jnp.int32(0)
+    for doc in range(lengths.shape[0]):
+        end = end + lengths[doc]
+        begins = jnp.where(places >= end, end, begins)
+    inside[...] = places - begins
+
+    pl.semaphore_wait(barrier, ctx_count + ch_count - 2)
+
+    send_rim = remote(
+        streams_hbm.at[:, pl.ds(tokens - 16, 16), :], rim, rim_sem.at[0], rim_sem.at[1],
+        ctx_at(1), my_ch,
+    )
+    send_rim.start()
+
     for load in loads[:3]:
         load.wait()
     filters = values.shape[3]
@@ -201,22 +217,6 @@
                     [parts[0][at : at + 8], parts[1][at : at + 8]], axis=0
                 ).astype(bf16)
 
-    begins = jnp.zeros((tokens, LANES), jnp.int32)
-    places = me * tokens + lax.broadcasted_iota(jnp.int32, (tokens, LANES), 0)
-    end = jnp.int32(0)
-    for doc in range(lengths.shape[0]):
-        end = end + lengths[doc]
-        begins = jnp.where(places >= end, end, begins)
-    inside[...] = places - begins
-
-    pl.semaphore_wait(barrier, ctx_count + ch_count - 2)
-
-    send_rim = remote(
-        streams_hbm.at[:, pl.ds(tokens - 16, 16), :], rim, rim_sem.at[0], rim_sem.at[1],
-        ctx_at(1), my_ch,
-    )
-    send_rim.start()
-
     def ch_copy(step):
         to = ch_at(step)
         return remote(
@@ -271,7 +271,7 @@
         feature(2, lanes, put_product)
 
     def order(index):
-        return 1 + lax.rem(index + 3, ctx_count - 1)
+        return 1 + index
 
     def go_copy(step):
         to = ctx_at(step)

time: 45.9 us -> 43.8 us (0.954)
  Pallas kernels: 43.9 us -> 41.7 us
    pallas_call x1, Pallas kernels: 43.9 us -> 41.7 us  [fused(): pl.pallas_call(functools.partial(block_kernel, ctx_count, ch_count), out_...]
where the time goes in v3:
time: 43.8 us; the launch traced here: 43.6 us
  Pallas kernels  41.7 us (95%)
  local copies, waits for them, and re-layouts  1.87 us (4%)
    pallas_call x1, Pallas kernels, fused(): pl.pallas_call(functools.partial(block_kernel, ctx_count, ch_count), out_...  41.7 us
    unnamed x1, local copies, waits for them, and re-layouts  1.87 us

profile of v3, /device:TPU:0, one launch (start us, length us, event | category | flops | bytes accessed | tf_op | source)
XLA Modules:
  0.0 43.6 jit_solution(3113082952358680797)
XLA Ops:
  0.0 41.7 %shard_map.91 = bf16[256,1024]{1,0:T(8,128)(2,1)} custom-call(bf16[3,256,1024]{2,1,0:T(8,128)(2,1)} %bitcast.3, s32[32]{0:T(128)} %lengths.1, f32[3,7,1024]{2,1,0:T(8,128)} %taps_hbm.1, f32[1,1024]{1,0:T(1,128)} %bitcast.4, bf16[2,2,256,128]{3,2,1,0:T(8,128)(2,1)} %values_hbm.1, f32[2,2,128]{2,1,0:T(2,128)} %scales_hbm.1, s32[1,256]{1,0:T(1,128)} %bitcast.5, ...), custom_call_target="tpu_custom_call" | custom-call | tf_op jit(solution)/shard_map/pallas_call | solution.py:499
  41.7 1.9 %copy.11 = bf16[256,1024]{1,0:T(8,128)(2,1)} copy(bf16[256,1024]{1,0:T(8,128)(2,1)} %shard_map.91) | data formatting | bytes 1048576
